TPU v7x, 256 devices: a whole 4x4x8 slice. The times are simulated.
256 devices in a mesh: dp: 4 (over z_lo), tile: 64 (over z_hi, x, y, core).
Axes of the slice: x: 4, y: 4, z: 8 (z_hi: 2, z_lo: 4; z = z_hi * 4 + z_lo), core: 2. Of those that a mesh axis runs over, the one named last changes fastest.
Arguments:
- query: bfloat16 [4, 24576, 1536], P('dp', 'tile'), may hold values from -6 to 6
- key: bfloat16 [4, 24576, 1536], P('dp', 'tile'), may hold values from -6 to 6
- value: bfloat16 [4, 24576, 1536], P('dp', 'tile'), may hold values from -6 to 6
- text_key: bfloat16 [4, 128, 1536], P('dp', 'tile'), may hold values from -6 to 6
- text_value: bfloat16 [4, 128, 1536], P('dp', 'tile'), may hold values from -6 to 6
- text_len: int32 [4], P('dp'), may hold values from 17 to 128
- window: int32 [4, 64, 2], P('dp'), may hold values 0 or 1
- query_gain: float32 [128], replicated, may hold values from 0.5 to 3
- key_gain: float32 [128], replicated, may hold values from 0.5 to 3
- grad_out: bfloat16 [4, 24576, 1536], P('dp', 'tile'), may hold values from -6 to 6
Outputs:
- attended: bfloat16 [4, 24576, 1536], P('dp', 'tile')
- grad_query: bfloat16 [4, 24576, 1536], P('dp', 'tile')
- grad_key: bfloat16 [4, 24576, 1536], P('dp', 'tile')
- grad_value: bfloat16 [4, 24576, 1536], P('dp', 'tile')
- grad_text_key: float32 [4, 128, 1536], P('dp', 'tile')
- grad_text_value: float32 [4, 128, 1536], P('dp', 'tile')
- grad_query_gain: float32 [128], replicated
- grad_key_gain: float32 [128], replicated
All inputs are finite; a program needn't handle non-finite values. No bound on the sum of `window` on one device may be relied on, other than what follows from the above.
Results may differ from a plain program's by a relative error of at most 0.012.
The roundings to bfloat16 on the way count: a program that leaves them out, or rounds other values in their place, can miss the bound.
Values may be sent and summed in bfloat16 or wider, within the bound.
No kernel may reach another device: no remote copies, remote signals or barrier semaphores. Data moves between devices by JAX's collectives and lax.ppermute only.
A program may use at most 128 MiB of HBM per device.

v0:
```python
import functools
import math

import jax
import jax.numpy as jnp
from jax import lax
from jax.experimental import pallas as pl
from jax.experimental.pallas import tpu as pltpu
from jax.sharding import PartitionSpec as P

HEADS = 12
HEAD = 128
TT = 384
TXT = 128
W = HEADS * HEAD
SPLIT = ((0, 6), (6, 12))
SCALE = HEAD ** (-0.5)
LEAD = 2
BIG = 1e30
F32 = jnp.float32
BF16 = jnp.bfloat16

SIZES = (2, 4, 4, 2)


def place_of(zh, x, y, c):
    return ((zh * 4 + x) * 4 + y) * 2 + c


def steps_along(dim, by):
    pairs = []
    for i in range(64):
        at = [i // 32, i // 8 % 4, i // 2 % 4, i % 2]
        to = list(at)
        to[dim] = (at[dim] + by) % SIZES[dim]
        pairs.append((i, place_of(*to)))
    return pairs


def nt(a, b):
    return lax.dot_general(a, b, (((1,), (1,)), ((), ())), preferred_element_type=F32)


def nn(a, b):
    return lax.dot_general(a, b, (((1,), (0,)), ((), ())), preferred_element_type=F32)


def normed(x, gain):
    x = x.astype(F32)
    inv = lax.rsqrt(jnp.mean(x * x, -1, keepdims=True) + 1e-06)
    hat = x * inv
    return x, inv, hat, (hat * gain).astype(BF16)


def attend_kernel(steps, last, flags, *refs):
    gain_ref = refs[-3]
    step = pl.program_id(0)

    def work():
        totals = [[], []]
        one, two = [attend_head(n, flags, refs, totals[n]) for n in range(2)]
        for _ in range(LEAD):
            next(one)
        alive = [one, two]
        while alive:
            for head in list(alive):
                if next(head, None) is None:
                    alive.remove(head)
        gains = totals[0][0] + totals[1][0]

        @pl.when(step == 0)
        def _():
            gain_ref[...] = gains + refs[11][...] if last else gains

        @pl.when(step > 0)
        def _():
            gain_ref[...] += gains

    if not last:
        work()
        return

    @pl.when(step < steps)
    def _():
        work()

    @pl.when(step == steps)
    def _():
        for ref in refs[-5:-3]:
            for i in range(8):
                for n in range(4):
                    ref[n, i] = jnp.broadcast_to(gain_ref[i : i + 1, :], (8, HEAD))


def attend_head(n, flags, refs, totals):
    q_ref, k_ref, v_ref, g_ref, in_ref, out_ref, t0_ref, t1_ref, keep_ref, qg_ref, kg_ref = refs[:11]
    att_ref, gq_ref, own_ref, din_ref, dout_ref, dt0_ref, dt1_ref, _, s_ref, p_ref = refs[-10:]
    cols = slice(n * HEAD, (n + 1) * HEAD)
    qg, kg = qg_ref[...], kg_ref[...]
    q, q_inv, q_hat, qn = normed(q_ref[:, cols], qg)
    scaled = qn.astype(F32) * (SCALE * math.log2(math.e))
    high = scaled.astype(BF16)
    low = (scaled - high.astype(F32)).astype(BF16)
    queries = jnp.concatenate([high, low], 1)
    inner, outer = flags[0] > 0, flags[1] > 0

    texts = [jnp.concatenate([t_ref[4 * n + 2 * i + j] for j in range(2) for t_ref in (t0_ref, t1_ref)], 0) for i in range(2)]
    raw = (in_ref[0, :, cols], k_ref[:, cols], out_ref[0, :, cols], texts[0])
    vals = (in_ref[1, :, cols], v_ref[:, cols], out_ref[1, :, cols], texts[1])
    rows = (TT, TT, TT, TXT)
    at = [pl.ds(b * TT, rows[b]) for b in range(4)]

    hats, keys, tops = [], [], []
    for b in range(4):
        _, _, hat, kn = normed(raw[b], kg)
        hats.append(hat)
        keys.append(kn)
        s = nt(jnp.concatenate([kn, kn], 1), queries)
        if b == 3:
            s = jnp.where(keep_ref[...] > 0, s, -BIG)
        s_ref[n, at[b], :] = s
        top = jnp.max(s, 0, keepdims=True)
        if b == 0:
            top = jnp.where(inner, top, -BIG)
        if b == 2:
            top = jnp.where(outer, top, -BIG)
        tops.append(top)
        yield 0
    top = jnp.maximum(jnp.maximum(tops[0], tops[1]), jnp.maximum(tops[2], tops[3]))
    total = jnp.zeros((1, TT), F32)
    for b in range(4):
        shift = top
        if b == 0:
            shift = jnp.where(inner, top, BIG)
        if b == 2:
            shift = jnp.where(outer, top, BIG)
        e = jnp.exp2(s_ref[n, at[b], :] - shift)
        s_ref[n, at[b], :] = e
        total += jnp.sum(e, 0, keepdims=True)
        yield 0
    part = 1.0 / total
    out = jnp.zeros((HEAD, TT), F32)
    for b in range(4):
        p16 = (s_ref[n, at[b], :] * part).astype(BF16)
        p_ref[n, at[b], :] = p16
        out += nn(vals[b].T, p16)
        yield 0
    att = out.T.astype(BF16)
    att_ref[:, cols] = att

    g = g_ref[:, cols]
    delta = jnp.sum(g.astype(F32) * att.astype(F32), -1, keepdims=True)
    lane = lax.broadcasted_iota(jnp.int32, (TT, HEAD), 1)
    d1 = delta.astype(BF16).astype(F32)
    d2 = (delta - d1).astype(BF16).astype(F32)
    d3 = delta - d1 - d2
    extra = jnp.where(lane == 0, -d1, jnp.where(lane == 1, -d2, jnp.where(lane == 2, -d3, 0.0)))
    cot = jnp.concatenate([g, extra.astype(BF16)], 1)
    dq = jnp.zeros((HEAD, TT), F32)
    gain_k = jnp.zeros((1, HEAD), F32)
    for b in range(4):
        ones = (lax.broadcasted_iota(jnp.int32, (rows[b], HEAD), 1) < 3).astype(F32).astype(BF16)
        dp = nt(jnp.concatenate([vals[b], ones], 1), cot)
        ds = (s_ref[n, at[b], :] * part * dp).astype(BF16)
        dv = nn(p_ref[n, at[b], :], g)
        dk = nn(ds, qn) * SCALE
        dq += nn(keys[b].T, ds)
        gain_k += jnp.sum(dk * hats[b], 0, keepdims=True)
        if b < 3:
            into = (din_ref, own_ref, dout_ref)[b]
            into[0, :, cols] = dk.astype(into.dtype)
            into[1, :, cols] = dv.astype(into.dtype)
        else:
            for i, x in enumerate((dk, dv)):
                for j in range(2):
                    for m in range(4):
                        first = j * 64 + m * 8
                        dt0_ref[m, 4 * n + 2 * i + j] = x[first : first + 8]
                        dt1_ref[m, 4 * n + 2 * i + j] = x[first + 32 : first + 40]
        yield 0
    dqn = dq.T * SCALE
    u = dqn * qg
    gq_ref[:, cols] = (q_inv * u - q_hat * (q_inv * q_inv) * jnp.mean(u * q, -1, keepdims=True)).astype(BF16)
    gain_q = jnp.sum(dqn * q_hat, 0, keepdims=True)
    row = lax.broadcasted_iota(jnp.int32, (8, HEAD), 0)
    totals.append(jnp.where(row == 0, gain_q, jnp.where(row == 1, gain_k, 0.0)))
    yield 0


def attend(chunk, flags, q, k, v, g, inner, outer, texts, keep, qg, kg, before):
    base, end = SPLIT[chunk]
    heads, last = end - base, before is not None
    steps, base = heads // 2, base // 2
    at = lambda h: jnp.minimum(h, steps - 1)
    wide = pl.BlockSpec((TT, 2 * HEAD), lambda h, f: (0, at(h) + base))
    pair = pl.BlockSpec((2, TT, 2 * HEAD), lambda h, f: (0, 0, at(h)))
    tall = pl.BlockSpec((8, 32, HEAD), lambda h, f: (at(h) + base, 0, 0))
    half = pl.BlockSpec((4, 8, 8, HEAD), lambda h, f: (0, h + base, 0, 0))
    whole = lambda *shape: pl.BlockSpec(shape, lambda h, f: (0,) * len(shape))
    in_specs = [wide] * 4 + [pair, pair, tall, tall, whole(TXT, 1), whole(1, HEAD), whole(1, HEAD)]
    args = [q, k, v, g, inner, outer, *texts, keep, qg, kg]
    aliases = {}
    if last:
        in_specs += [whole(8, HEAD)] + [pl.BlockSpec(memory_space=pl.ANY)] * 4
        aliases = {len(args) + 2: 0, len(args) + 3: 1, len(args) + 4: 5, len(args) + 5: 6}
        args += [before[7], before[0], before[1], before[5], before[6]]
    size = (3 * TT + TXT) * TT * heads
    width = heads * HEAD
    return pl.pallas_call(
        functools.partial(attend_kernel, steps, last),
        grid_spec=pltpu.PrefetchScalarGridSpec(
            num_scalar_prefetch=1,
            grid=(steps + last,),
            in_specs=in_specs,
            out_specs=[wide, wide, pair, pair, pair, half, half, whole(8, HEAD)],
            scratch_shapes=[
                pltpu.VMEM((2, 3 * TT + TXT, TT), F32),
                pltpu.VMEM((2, 3 * TT + TXT, TT), BF16),
            ],
        ),
        out_shape=[
            jax.ShapeDtypeStruct((TT, W), BF16),
            jax.ShapeDtypeStruct((TT, W), BF16),
            jax.ShapeDtypeStruct((2, TT, width), F32),
            jax.ShapeDtypeStruct((2, TT, width), BF16),
            jax.ShapeDtypeStruct((2, TT, width), BF16),
            jax.ShapeDtypeStruct((4, 4 * HEADS + 8, 8, HEAD), F32),
            jax.ShapeDtypeStruct((4, 4 * HEADS + 8, 8, HEAD), F32),
            jax.ShapeDtypeStruct((8, HEAD), F32),
        ],
        input_output_aliases=aliases,
        compiler_params=pltpu.CompilerParams(vmem_limit_bytes=60 * 2**20),
        cost_estimate=pl.CostEstimate(flops=24 * HEAD * size, bytes_accessed=18 * TT * width, transcendentals=size),
    )(flags, *args)


def finish_kernel(k_ref, own_ref, a_ref, b_ref, kg_ref, *rest):
    gk_ref, gv_ref = rest[-2:]
    for n in range(2):
        cols = slice(n * HEAD, (n + 1) * HEAD)
        k, inv, hat, _ = normed(k_ref[:, cols], kg_ref[...])
        dk, dv = [own_ref[i, :, cols] + a_ref[i, :, cols].astype(F32) + b_ref[i, :, cols].astype(F32) for i in range(2)]
        u = dk * kg_ref[...]
        gk_ref[:, cols] = (inv * u - hat * (inv * inv) * jnp.mean(u * k, -1, keepdims=True)).astype(BF16)
        gv_ref[:, cols] = dv.astype(BF16)


def finish(chunk, k, own, a, b, kg, before):
    base, end = SPLIT[chunk]
    heads = end - base
    wide = pl.BlockSpec((TT, 2 * HEAD), lambda h: (0, h + base // 2))
    pair = pl.BlockSpec((2, TT, 2 * HEAD), lambda h: (0, 0, h))
    in_specs = [wide, pair, pair, pair, pl.BlockSpec((1, HEAD), lambda h: (0, 0))]
    args = [k, own, a, b, kg]
    aliases = {}
    if before is not None:
        aliases = {len(args): 0, len(args) + 1: 1}
        in_specs += [pl.BlockSpec(memory_space=pl.ANY)] * 2
        args += list(before)
    return pl.pallas_call(
        finish_kernel,
        grid=(heads // 2,),
        in_specs=in_specs,
        out_specs=[wide, wide],
        out_shape=[jax.ShapeDtypeStruct((TT, W), BF16)] * 2,
        input_output_aliases=aliases,
        compiler_params=pltpu.CompilerParams(vmem_limit_bytes=60 * 2**20),
        cost_estimate=pl.CostEstimate(flops=20 * TT * heads * HEAD, bytes_accessed=26 * TT * heads * HEAD, transcendentals=TT),
    )(*args)


def send(x, pairs):
    return lax.ppermute(x, "tile", pairs)


INNER = [(i, i ^ 1) for i in range(64)]
OUTER = [(i, (i - 1 ^ 1) + 1) for i in range(1, 63)]


def after(x, *others):
    for other in others:
        zero = jnp.minimum(jnp.abs(other[(-1,) * other.ndim]), 0).astype(x.dtype)
        x = x + zero
    return x


def gather_all(x, packs):
    x = x[None]
    got = send(x, steps_along(0, 1))
    pack = after(packs[0], got)
    inners, outers = [send(pack, INNER)], [send(pack, OUTER)]
    x = jnp.concatenate([x, got], 0)
    stage = [send(x, steps_along(1, by)) for by in range(1, 4)]
    x = jnp.stack([x] + stage)
    stage = [send(x, steps_along(2, by)) for by in range(1, 4)]
    x = jnp.stack([x] + stage)
    pack = after(packs[1], *stage)
    inners.append(send(pack, INNER))
    outers.append(send(pack, OUTER))
    x = x.transpose(3, 1, 0, 2, 4).reshape(4 * HEADS, 32, HEAD)
    return (x, send(x, steps_along(3, 1))), inners, outers


def reduce_text(mine, other, first, second):
    total = mine + send(other, steps_along(3, -1))
    for dim in (1, 2, 0):
        if dim == 1:
            parts = [total[i] for i in range(4)]
        else:
            total = after(total, *(first if dim == 2 else second))
            n = total.shape[1] // SIZES[dim]
            parts = [total[:, i * n : (i + 1) * n] for i in range(SIZES[dim])]
        got = [send(parts[by], steps_along(dim, -by)) for by in range(1, SIZES[dim])]
        total = functools.reduce(jnp.add, got, parts[0])
    return total[:, 0]


def per_device(query, key, value, text_key, text_value, text_len, window, query_gain, key_gain, grad_out):
    me = lax.axis_index("tile")
    q, k, v, g = query[0], key[0], value[0], grad_out[0]
    bits = lax.dynamic_index_in_dim(window[0], me, 0, keepdims=False)
    below, above = (bits[0] > 0) & (me > 0), (bits[1] > 0) & (me < 63)
    even = me % 2 == 0
    flags = jnp.stack([jnp.where(even, above, below), jnp.where(even, below, above)]).astype(jnp.int32)
    qg, kg = query_gain.reshape(1, HEAD), key_gain.reshape(1, HEAD)

    rows = jnp.stack([text_key[0], text_value[0]]).reshape(2, 2, HEADS, HEAD).transpose(2, 0, 1, 3).reshape(4 * HEADS, HEAD)
    packs = [jnp.stack([k[:, a * HEAD : b * HEAD], v[:, a * HEAD : b * HEAD]]) for a, b in SPLIT]
    texts, inners, outers = gather_all(rows, packs)
    slot = jnp.arange(64)
    here = (me // 32, me // 8 % 4, me // 2 % 4, me % 2)
    back = (slot % 2, slot // 8 % 4, slot // 2 % 4, slot // 32)
    owner = place_of(*[(m - b) % s for m, b, s in zip(here, back, SIZES)])
    index = (owner[None, :] * 2 + jnp.arange(2)[:, None]).reshape(TXT, 1)
    keep = (index < text_len[0]).astype(F32)

    outs, parts = None, []
    for c in range(len(SPLIT)):
        outs = attend(c, flags, q, k, v, g, inners[c], outers[c], texts, keep, qg, kg, outs)
        own, din, dout = outs[2:5]
        parts.append((own, send(din, INNER), send(dout, OUTER)))
    fins = finish(0, k, *parts[0], kg, None)
    summed = reduce_text(outs[5], outs[6], [fins[1][:1, :1]], parts[1][1:])
    fins = finish(1, k, *parts[1], kg, fins)

    gains = summed[4 * HEADS : 4 * HEADS + 2]
    total = gains
    for by in range(1, 4):
        total = total + lax.ppermute(gains, "dp", [(i, (i + by) % 4) for i in range(4)])
    dtn, dtv = [summed[: 4 * HEADS].reshape(HEADS, 2, 2, HEAD)[:, i].transpose(1, 0, 2) for i in range(2)]
    t = text_key[0].astype(F32).reshape(2, HEADS, HEAD)
    inv = lax.rsqrt(jnp.mean(t * t, -1, keepdims=True) + 1e-06)
    u = dtn * key_gain
    gtk = (inv * u - t * inv**3 * jnp.mean(u * t, -1, keepdims=True)).reshape(1, 2, W)
    return (
        outs[0][None],
        outs[1][None],
        fins[0][None],
        fins[1][None],
        gtk,
        dtv.reshape(1, 2, W),
        total[0],
        total[1],
    )


def solution(mesh):
    row = P("dp", "tile", None)
    in_specs = (row, row, row, row, row, P("dp"), P("dp", None, None), P(), P(), row)
    out_specs = (row, row, row, row, row, row, P(), P())
    return jax.shard_map(per_device, mesh=mesh, in_specs=in_specs, out_specs=out_specs, check_vma=False)
```

profile of v0, /device:TPU:31, one launch (start us, length us, event | category | flops | bytes accessed | tf_op | source)
XLA Modules:
  0.0 164.3 jit_solution(7044608808533649877)
XLA Ops:
  1.4 7.0 %collective-permute-start = (bf16[1,48,128]{2,1,0:T(8,128)(2,1)S(1)}, bf16[1,48,128]{2,1,0:T(8,128)(2,1)S(1)}, u32[]{:S(2)}, u32[]{:S(2)}) collective-permute-start(bf16[1,48,128]{2,1,0:T(8,128)(2,1)S(1)} %bitcast.117), channel_id=1, source_target_pairs={{0,32},{1,33},{2,34},{3,35},{4,36},{5,37},{6,38},{7,39},{8,40},{9,... | collective-permute-start | bytes 36872 | tf_op jit(solution)/shard_map/ppermute | solution.py:273
  8.4 1.8 %slice_bitcast_fusion = (bf16[1,384,768]{2,1,0:T(8,128)(2,1)S(1)}, bf16[1,384,768]{2,1,0:T(8,128)(2,1)S(1)}, bf16[1,384,768]{2,1,0:T(8,128)(2,1)S(1)}, bf16[1,384,768]{2,1,0:T(8,128)(2,1)S(1)}) fusion(bf16[384,1536]{1,0:T(8,128)(2,1)} %bitcast.106, bf16[384,1536]{1,0:T(8,128)(2,1)} %bitcast.100), kind=kLoop, calls=%fused_computation.4 | loop fusion | bytes 4718592 | tf_op jit(solution)/shard_map/stack | solution.py:328
  11.6 7.9 %collective-permute-start.11 = (bf16[2,384,768]{2,1,0:T(8,128)(2,1)S(1)}, bf16[2,384,768]{2,1,0:T(8,128)(2,1)}, u32[]{:S(2)}, u32[]{:S(2)}) collective-permute-start(bf16[2,384,768]{2,1,0:T(8,128)(2,1)S(1)} %maximum_add_fusion.1), channel_id=1, source_target_pairs={{1,2},{2,1},{3,4},{4,3},{5,6},{6,5},{7,8},{8,7},{9,10},{10,9},{11,... | collective-permute-start | bytes 3538952 | tf_op jit(solution)/shard_map/ppermute | solution.py:273
  19.8 1.5 collective-permute-start.3
  23.9 6.2 %collective-permute-done.1 = bf16[2,48,128]{2,1,0:T(8,128)(2,1)S(1)} collective-permute-done((bf16[2,48,128]{2,1,0:T(8,128)(2,1)S(1)}, bf16[2,48,128]{2,1,0:T(8,128)(2,1)S(1)}, u32[]{:S(2)}, u32[]{:S(2)}) %collective-permute-start.1) | collective-permute-done | bytes 24608 | tf_op jit(solution)/shard_map/ppermute | solution.py:273
  30.3 2.6 %collective-permute-start.4 = (bf16[4,2,48,128]{3,2,1,0:T(8,128)(2,1)S(1)}, bf16[4,2,48,128]{3,2,1,0:T(8,128)(2,1)S(1)}, u32[]{:S(2)}, u32[]{:S(2)}) collective-permute-start(bf16[4,2,48,128]{3,2,1,0:T(8,128)(2,1)S(1)} %get-tuple-element.59), channel_id=1, source_target_pairs={{0,2},{1,3},{2,4},{3,5},{4,6},{5,7},{6,0},{7,1},{8,10},{9,11},{10,... | collective-permute-start | bytes 294920 | tf_op jit(solution)/shard_map/ppermute | solution.py:273
  32.9 9.2 %collective-permute-done.6 = bf16[4,2,48,128]{3,2,1,0:T(8,128)(2,1)S(1)} collective-permute-done((bf16[4,2,48,128]{3,2,1,0:T(8,128)(2,1)S(1)}, bf16[4,2,48,128]{3,2,1,0:T(8,128)(2,1)S(1)}, u32[]{:S(2)}, u32[]{:S(2)}) %collective-permute-start.6) | collective-permute-done | bytes 98336 | tf_op jit(solution)/shard_map/ppermute | solution.py:273
  47.4 8.9 %collective-permute-start.8 = (bf16[2,384,768]{2,1,0:T(8,128)(2,1)S(1)}, bf16[2,384,768]{2,1,0:T(8,128)(2,1)}, u32[]{:S(2)}, u32[]{:S(2)}) collective-permute-start(bf16[2,384,768]{2,1,0:T(8,128)(2,1)S(1)} %fusion.1), channel_id=1, source_target_pairs={{1,2},{2,1},{3,4},{4,3},{5,6},{6,5},{7,8},{8,7},{9,10},{10,9},{11,... | collective-permute-start | bytes 3538952 | tf_op jit(solution)/shard_map/ppermute | solution.py:273
  58.0 19.4 %shard_map.161 = (bf16[384,1536]{1,0:T(8,128)(2,1)}, bf16[384,1536]{1,0:T(8,128)(2,1)}, f32[2,384,768]{2,1,0:T(8,128)}, bf16[2,384,768]{2,1,0:T(8,128)(2,1)}, bf...) custom-call(s32[2]{0:T(128)} %add_convert_fusion.flags, ...), custom_call_target="tpu_custom_call" | custom-call | flops 9059696640 | bytes 5308416 | tf_op jit(solution)/shard_map/pallas_call | solution.py:209
  78.0 4.8 %collective-permute-start.15 = (bf16[2,384,768]{2,1,0:T(8,128)(2,1)}, bf16[2,384,768]{2,1,0:T(8,128)(2,1)}, u32[]{:S(2)}, u32[]{:S(2)}) collective-permute-start(bf16[2,384,768]{2,1,0:T(8,128)(2,1)} %get-tuple-element.39), channel_id=1, source_target_pairs={{1,2},{2,1},{3,4},{4,3},{5,6},{6,5},{7,8},{8,7},{9,10},{10,9},{11,... | collective-permute-start | bytes 3538952 | tf_op jit(solution)/shard_map/ppermute | solution.py:273
  82.8 19.6 %shard_map.162 = (bf16[384,1536]{1,0:T(8,128)(2,1)}, bf16[384,1536]{1,0:T(8,128)(2,1)}, f32[2,384,768]{2,1,0:T(8,128)}, bf16[2,384,768]{2,1,0:T(8,128)(2,1)}, bf...) custom-call(s32[2]{0:T(128)} %add_convert_fusion.flags, ...), custom_call_target="tpu_custom_call", output_to_operand_aliasing={{0}: (13, {}), {1}: (14, {}), {5}: (15, {}), {6}: (16, {})} | custom-call | flops 9059696640 | bytes 5308416 | tf_op jit(solution)/shard_map/pallas_call | solution.py:209
  103.0 8.9 %collective-permute-start.13 = (bf16[2,384,768]{2,1,0:T(8,128)(2,1)}, bf16[2,384,768]{2,1,0:T(8,128)(2,1)S(1)}, u32[]{:S(2)}, u32[]{:S(2)}) collective-permute-start(bf16[2,384,768]{2,1,0:T(8,128)(2,1)} %get-tuple-element.36), channel_id=1, source_target_pairs={{1,2},{2,1},{3,4},{4,3},{5,6},{6,5},{7,8},{8,7},{9,10},{10,9},{11,... | collective-permute-start | bytes 3538952 | tf_op jit(solution)/shard_map/ppermute | solution.py:273
  111.9 1.3 add.246
  114.1 2.7 %collective-permute-start.19 = (f32[56,8,128]{2,1,0:T(8,128)}, f32[56,8,128]{2,1,0:T(8,128)}, u32[]{:S(2)}, u32[]{:S(2)}) collective-permute-start(f32[56,8,128]{2,1,0:T(8,128)} %get-tuple-element.53), channel_id=1, source_target_pairs={{0,8},{1,9},{2,10},{3,11},{4,12},{5,13},{6,14},{7,15},{8,16},{9,17... | collective-permute-start | bytes 688136 | tf_op jit(solution)/shard_map/ppermute | solution.py:273
  116.8 4.6 %shard_map.163 = (bf16[384,1536]{1,0:T(8,128)(2,1)}, bf16[384,1536]{1,0:T(8,128)(2,1)}) custom-call(bf16[384,1536]{1,0:T(8,128)(2,1)} %bitcast.103, f32[2,384,768]{2,1,0:T(8,128)} %get-tuple-element.37.own_ref, bf16[2,384,768]{2,1,0:T(8,128)(2,1)} %collective-permute-done.14.a_ref, bf16[2,384,768]{2,1,0:T(8,128)(2,1)} %collective-permute-done.15.b_ref, ...), custom_call_target="tpu_custom_call" | custom-call | flops 5898240 | bytes 7667712 | tf_op jit(solution)/shard_map/pallas_call | solution.py:260
  124.0 1.2 fusion.5
  125.4 2.7 %collective-permute-start.22 = (f32[56,2,128]{2,1,0:T(2,128)S(1)}, f32[56,2,128]{2,1,0:T(2,128)S(1)}, u32[]{:S(2)}, u32[]{:S(2)}) collective-permute-start(f32[56,2,128]{2,1,0:T(2,128)S(1)} %get-tuple-element.56), channel_id=1, source_target_pairs={{0,2},{1,3},{2,4},{3,5},{4,6},{5,7},{6,0},{7,1},{8,10},{9,11},{10,... | collective-permute-start | bytes 172040 | tf_op jit(solution)/shard_map/ppermute | solution.py:273
  129.4 2.2 %collective-permute-done.13.b_ref = bf16[2,384,768]{2,1,0:T(8,128)(2,1)S(1)} collective-permute-done((bf16[2,384,768]{2,1,0:T(8,128)(2,1)}, bf16[2,384,768]{2,1,0:T(8,128)(2,1)S(1)}, u32[]{:S(2)}, u32[]{:S(2)}) %collective-permute-start.13) | collective-permute-done | bytes 1179680 | tf_op jit(solution)/shard_map/ppermute | solution.py:273
  133.8 4.7 %shard_map.164 = (bf16[384,1536]{1,0:T(8,128)(2,1)}, bf16[384,1536]{1,0:T(8,128)(2,1)}) custom-call(bf16[384,1536]{1,0:T(8,128)(2,1)} %bitcast.104, f32[2,384,768]{2,1,0:T(8,128)} %get-tuple-element.34.own_ref, bf16[2,384,768]{2,1,0:T(8,128)(2,1)} %copy-done.1, bf16[2,384,768]{2,1,0:T(8,128)(2,1)} %copy-done.2, ...), custom_call_target="tpu_custom_call", output_to_operand_aliasing={{0}: (5, {}), {1}: (6, {})} | custom-call | flops 5898240 | bytes 7667712 | tf_op jit(solution)/shard_map/pallas_call | solution.py:260
  138.5 8.6 %collective-permute-done.23 = f32[56,1,128]{2,1,0:T(1,128)S(1)} collective-permute-done((f32[56,1,128]{2,1,0:T(1,128)S(1)}, f32[56,1,128]{2,1,0:T(1,128)S(1)}, u32[]{:S(2)}, u32[]{:S(2)}) %collective-permute-start.23) | collective-permute-done | bytes 28704 | tf_op jit(solution)/shard_map/ppermute | solution.py:273
  147.1 2.2 %collective-permute-start.26 = (f32[2,128]{1,0:T(2,128)S(1)}, f32[2,128]{1,0:T(2,128)S(1)}, u32[]{:S(2)}, u32[]{:S(2)}) collective-permute-start(f32[2,128]{1,0:T(2,128)S(1)} %bitcast.126), channel_id=1, source_target_pairs={{0,192},{64,0},{128,64},{192,128},{1,193},{65,1},{129,65},{193,129... | collective-permute-start | bytes 3080 | tf_op jit(solution)/shard_map/ppermute | solution.py:349
  149.3 10.2 %collective-permute-start.25 = (f32[2,128]{1,0:T(2,128)S(1)}, f32[2,128]{1,0:T(2,128)S(1)}, u32[]{:S(2)}, u32[]{:S(2)}) collective-permute-start(f32[2,128]{1,0:T(2,128)S(1)} %bitcast.127), channel_id=1, source_target_pairs={{0,128},{64,192},{128,0},{192,64},{1,129},{65,193},{129,1},{193,65... | collective-permute-start | bytes 3080 | tf_op jit(solution)/shard_map/ppermute | solution.py:349
  159.5 1.4 collective-permute-start.24
  162.3 1.4 collective-permute-done.24
  (90 shorter events, 15.9 us)
Async XLA Ops:
  1.4 8.8 %collective-permute-start = (bf16[1,48,128]{2,1,0:T(8,128)(2,1)S(1)}, bf16[1,48,128]{2,1,0:T(8,128)(2,1)S(1)}, u32[]{:S(2)}, u32[]{:S(2)}) collective-permute-start(bf16[1,48,128]{2,1,0:T(8,128)(2,1)S(1)} %bitcast.117), channel_id=1, source_target_pairs={{0,32},{1,33},{2,34},{3,35},{4,36},{5,37},{6,38},{7,39},{8,40},{9,... | collective-permute-start | bytes 36872 | tf_op jit(solution)/shard_map/ppermute | solution.py:273
  11.6 46.4 %collective-permute-start.11 = (bf16[2,384,768]{2,1,0:T(8,128)(2,1)S(1)}, bf16[2,384,768]{2,1,0:T(8,128)(2,1)}, u32[]{:S(2)}, u32[]{:S(2)}) collective-permute-start(bf16[2,384,768]{2,1,0:T(8,128)(2,1)S(1)} %maximum_add_fusion.1), channel_id=1, source_target_pairs={{1,2},{2,1},{3,4},{4,3},{5,6},{6,5},{7,8},{8,7},{9,10},{10,9},{11,... | collective-permute-start | bytes 3538952 | tf_op jit(solution)/shard_map/ppermute | solution.py:273
  19.4 38.5 %collective-permute-start.10 = (bf16[2,384,768]{2,1,0:T(8,128)(2,1)S(1)}, bf16[2,384,768]{2,1,0:T(8,128)(2,1)}, u32[]{:S(2)}, u32[]{:S(2)}) collective-permute-start(bf16[2,384,768]{2,1,0:T(8,128)(2,1)S(1)} %maximum_add_fusion.1), channel_id=1, source_target_pairs={{0,1},{1,0},{2,3},{3,2},{4,5},{5,4},{6,7},{7,6},{8,9},{9,8},{10,11... | collective-permute-start | bytes 3538952 | tf_op jit(solution)/shard_map/ppermute | solution.py:273
  19.7 10.4 %collective-permute-start.1 = (bf16[2,48,128]{2,1,0:T(8,128)(2,1)S(1)}, bf16[2,48,128]{2,1,0:T(8,128)(2,1)S(1)}, u32[]{:S(2)}, u32[]{:S(2)}) collective-permute-start(bf16[2,48,128]{2,1,0:T(8,128)(2,1)S(1)} %get-tuple-element.63), channel_id=1, source_target_pairs={{0,8},{1,9},{2,10},{3,11},{4,12},{5,13},{6,14},{7,15},{8,16},{9,17... | collective-permute-start | bytes 73736 | tf_op jit(solution)/shard_map/ppermute | solution.py:273
  19.8 10.3 %collective-permute-start.3 = (bf16[2,48,128]{2,1,0:T(8,128)(2,1)S(1)}, bf16[2,48,128]{2,1,0:T(8,128)(2,1)S(1)}, u32[]{:S(2)}, u32[]{:S(2)}) collective-permute-start(bf16[2,48,128]{2,1,0:T(8,128)(2,1)S(1)} %get-tuple-element.63), channel_id=1, source_target_pairs={{0,24},{1,25},{2,26},{3,27},{4,28},{5,29},{6,30},{7,31},{8,0},{9,1... | collective-permute-start | bytes 73736 | tf_op jit(solution)/shard_map/ppermute | solution.py:273
  30.1 11.9 %collective-permute-start.6 = (bf16[4,2,48,128]{3,2,1,0:T(8,128)(2,1)S(1)}, bf16[4,2,48,128]{3,2,1,0:T(8,128)(2,1)S(1)}, u32[]{:S(2)}, u32[]{:S(2)}) collective-permute-start(bf16[4,2,48,128]{3,2,1,0:T(8,128)(2,1)S(1)} %get-tuple-element.59), channel_id=1, source_target_pairs={{0,6},{1,7},{2,0},{3,1},{4,2},{5,3},{6,4},{7,5},{8,14},{9,15},{10,... | collective-permute-start | bytes 294920 | tf_op jit(solution)/shard_map/ppermute | solution.py:273
  30.2 13.1 %collective-permute-start.5 = (bf16[4,2,48,128]{3,2,1,0:T(8,128)(2,1)S(1)}, bf16[4,2,48,128]{3,2,1,0:T(8,128)(2,1)S(1)}, u32[]{:S(2)}, u32[]{:S(2)}) collective-permute-start(bf16[4,2,48,128]{3,2,1,0:T(8,128)(2,1)S(1)} %get-tuple-element.59), channel_id=1, source_target_pairs={{0,4},{1,5},{2,6},{3,7},{4,0},{5,1},{6,2},{7,3},{8,12},{9,13},{10,... | collective-permute-start | bytes 294920 | tf_op jit(solution)/shard_map/ppermute | solution.py:273
  30.3 14.3 %collective-permute-start.4 = (bf16[4,2,48,128]{3,2,1,0:T(8,128)(2,1)S(1)}, bf16[4,2,48,128]{3,2,1,0:T(8,128)(2,1)S(1)}, u32[]{:S(2)}, u32[]{:S(2)}) collective-permute-start(bf16[4,2,48,128]{3,2,1,0:T(8,128)(2,1)S(1)} %get-tuple-element.59), channel_id=1, source_target_pairs={{0,2},{1,3},{2,4},{3,5},{4,6},{5,7},{6,0},{7,1},{8,10},{9,11},{10,... | collective-permute-start | bytes 294920 | tf_op jit(solution)/shard_map/ppermute | solution.py:273
  46.7 11.2 %collective-permute-start.9 = (bf16[48,32,128]{2,1,0:T(8,128)(2,1)}, bf16[48,32,128]{2,1,0:T(8,128)(2,1)}, u32[]{:S(2)}, u32[]{:S(2)}) collective-permute-start(bf16[48,32,128]{2,1,0:T(8,128)(2,1)} %copy.36.refs_6_), channel_id=1, source_target_pairs={{0,1},{1,0},{2,3},{3,2},{4,5},{5,4},{6,7},{7,6},{8,9},{9,8},{10,11... | collective-permute-start | bytes 1179656 | tf_op jit(solution)/shard_map/ppermute | solution.py:273
  47.4 35.4 %collective-permute-start.8 = (bf16[2,384,768]{2,1,0:T(8,128)(2,1)S(1)}, bf16[2,384,768]{2,1,0:T(8,128)(2,1)}, u32[]{:S(2)}, u32[]{:S(2)}) collective-permute-start(bf16[2,384,768]{2,1,0:T(8,128)(2,1)S(1)} %fusion.1), channel_id=1, source_target_pairs={{1,2},{2,1},{3,4},{4,3},{5,6},{6,5},{7,8},{8,7},{9,10},{10,9},{11,... | collective-permute-start | bytes 3538952 | tf_op jit(solution)/shard_map/ppermute | solution.py:273
  56.2 26.5 %collective-permute-start.7 = (bf16[2,384,768]{2,1,0:T(8,128)(2,1)S(1)}, bf16[2,384,768]{2,1,0:T(8,128)(2,1)}, u32[]{:S(2)}, u32[]{:S(2)}) collective-permute-start(bf16[2,384,768]{2,1,0:T(8,128)(2,1)S(1)} %fusion.1), channel_id=1, source_target_pairs={{0,1},{1,0},{2,3},{3,2},{4,5},{5,4},{6,7},{7,6},{8,9},{9,8},{10,11... | collective-permute-start | bytes 3538952 | tf_op jit(solution)/shard_map/ppermute | solution.py:273
  77.4 36.7 %collective-permute-start.14 = (bf16[2,384,768]{2,1,0:T(8,128)(2,1)}, bf16[2,384,768]{2,1,0:T(8,128)(2,1)}, u32[]{:S(2)}, u32[]{:S(2)}) collective-permute-start(bf16[2,384,768]{2,1,0:T(8,128)(2,1)} %get-tuple-element.38), channel_id=1, source_target_pairs={{0,1},{1,0},{2,3},{3,2},{4,5},{5,4},{6,7},{7,6},{8,9},{9,8},{10,11... | collective-permute-start | bytes 3538952 | tf_op jit(solution)/shard_map/ppermute | solution.py:273
  78.0 38.8 %collective-permute-start.15 = (bf16[2,384,768]{2,1,0:T(8,128)(2,1)}, bf16[2,384,768]{2,1,0:T(8,128)(2,1)}, u32[]{:S(2)}, u32[]{:S(2)}) collective-permute-start(bf16[2,384,768]{2,1,0:T(8,128)(2,1)} %get-tuple-element.39), channel_id=1, source_target_pairs={{1,2},{2,1},{3,4},{4,3},{5,6},{6,5},{7,8},{8,7},{9,10},{10,9},{11,... | collective-permute-start | bytes 3538952 | tf_op jit(solution)/shard_map/ppermute | solution.py:273
  102.4 9.5 %collective-permute-start.16 = (f32[4,56,8,128]{3,2,1,0:T(8,128)}, f32[4,56,8,128]{3,2,1,0:T(8,128)S(1)}, u32[]{:S(2)}, u32[]{:S(2)}) collective-permute-start(f32[4,56,8,128]{3,2,1,0:T(8,128)} %get-tuple-element.45), channel_id=1, source_target_pairs={{0,1},{1,0},{2,3},{3,2},{4,5},{5,4},{6,7},{7,6},{8,9},{9,8},{10,11... | collective-permute-start | bytes 2752520 | tf_op jit(solution)/shard_map/ppermute | solution.py:273
  102.5 25.5 %collective-permute-start.12 = (bf16[2,384,768]{2,1,0:T(8,128)(2,1)}, bf16[2,384,768]{2,1,0:T(8,128)(2,1)S(1)}, u32[]{:S(2)}, u32[]{:S(2)}) collective-permute-start(bf16[2,384,768]{2,1,0:T(8,128)(2,1)} %get-tuple-element.35), channel_id=1, source_target_pairs={{0,1},{1,0},{2,3},{3,2},{4,5},{5,4},{6,7},{7,6},{8,9},{9,8},{10,11... | collective-permute-start | bytes 3538952 | tf_op jit(solution)/shard_map/ppermute | solution.py:273
  103.0 28.6 %collective-permute-start.13 = (bf16[2,384,768]{2,1,0:T(8,128)(2,1)}, bf16[2,384,768]{2,1,0:T(8,128)(2,1)S(1)}, u32[]{:S(2)}, u32[]{:S(2)}) collective-permute-start(bf16[2,384,768]{2,1,0:T(8,128)(2,1)} %get-tuple-element.36), channel_id=1, source_target_pairs={{1,2},{2,1},{3,4},{4,3},{5,6},{6,5},{7,8},{8,7},{9,10},{10,9},{11,... | collective-permute-start | bytes 3538952 | tf_op jit(solution)/shard_map/ppermute | solution.py:273
  114.1 9.2 %collective-permute-start.17 = (f32[56,8,128]{2,1,0:T(8,128)}, f32[56,8,128]{2,1,0:T(8,128)S(1)}, u32[]{:S(2)}, u32[]{:S(2)}) collective-permute-start(f32[56,8,128]{2,1,0:T(8,128)} %get-tuple-element.52), channel_id=1, source_target_pairs={{0,24},{1,25},{2,26},{3,27},{4,28},{5,29},{6,30},{7,31},{8,0},{9,1... | collective-permute-start | bytes 688136 | tf_op jit(solution)/shard_map/ppermute | solution.py:273
  114.1 9.2 %collective-permute-start.19 = (f32[56,8,128]{2,1,0:T(8,128)}, f32[56,8,128]{2,1,0:T(8,128)}, u32[]{:S(2)}, u32[]{:S(2)}) collective-permute-start(f32[56,8,128]{2,1,0:T(8,128)} %get-tuple-element.53), channel_id=1, source_target_pairs={{0,8},{1,9},{2,10},{3,11},{4,12},{5,13},{6,14},{7,15},{8,16},{9,17... | collective-permute-start | bytes 688136 | tf_op jit(solution)/shard_map/ppermute | solution.py:273
  116.8 7.2 %collective-permute-start.18 = (f32[56,8,128]{2,1,0:T(8,128)}, f32[56,8,128]{2,1,0:T(8,128)}, u32[]{:S(2)}, u32[]{:S(2)}) collective-permute-start(f32[56,8,128]{2,1,0:T(8,128)} %get-tuple-element.54), channel_id=1, source_target_pairs={{0,16},{1,17},{2,18},{3,19},{4,20},{5,21},{6,22},{7,23},{8,24},{9,... | collective-permute-start | bytes 688136 | tf_op jit(solution)/shard_map/ppermute | solution.py:273
  125.3 8.2 %collective-permute-start.20 = (f32[56,2,128]{2,1,0:T(2,128)S(1)}, f32[56,2,128]{2,1,0:T(2,128)S(1)}, u32[]{:S(2)}, u32[]{:S(2)}) collective-permute-start(f32[56,2,128]{2,1,0:T(2,128)S(1)} %get-tuple-element.55), channel_id=1, source_target_pairs={{0,6},{1,7},{2,0},{3,1},{4,2},{5,3},{6,4},{7,5},{8,14},{9,15},{10,... | collective-permute-start | bytes 172040 | tf_op jit(solution)/shard_map/ppermute | solution.py:273
  125.4 8.1 %collective-permute-start.22 = (f32[56,2,128]{2,1,0:T(2,128)S(1)}, f32[56,2,128]{2,1,0:T(2,128)S(1)}, u32[]{:S(2)}, u32[]{:S(2)}) collective-permute-start(f32[56,2,128]{2,1,0:T(2,128)S(1)} %get-tuple-element.56), channel_id=1, source_target_pairs={{0,2},{1,3},{2,4},{3,5},{4,6},{5,7},{6,0},{7,1},{8,10},{9,11},{10,... | collective-permute-start | bytes 172040 | tf_op jit(solution)/shard_map/ppermute | solution.py:273
  133.6 13.4 %collective-permute-start.23 = (f32[56,1,128]{2,1,0:T(1,128)S(1)}, f32[56,1,128]{2,1,0:T(1,128)S(1)}, u32[]{:S(2)}, u32[]{:S(2)}) collective-permute-start(f32[56,1,128]{2,1,0:T(1,128)S(1)} %slice.143), channel_id=1, source_target_pairs={{0,32},{1,33},{2,34},{3,35},{4,36},{5,37},{6,38},{7,39},{8,40},{9,... | collective-permute-start | bytes 86024 | tf_op jit(solution)/shard_map/ppermute | solution.py:273
  147.1 15.2 %collective-permute-start.26 = (f32[2,128]{1,0:T(2,128)S(1)}, f32[2,128]{1,0:T(2,128)S(1)}, u32[]{:S(2)}, u32[]{:S(2)}) collective-permute-start(f32[2,128]{1,0:T(2,128)S(1)} %bitcast.126), channel_id=1, source_target_pairs={{0,192},{64,0},{128,64},{192,128},{1,193},{65,1},{129,65},{193,129... | collective-permute-start | bytes 3080 | tf_op jit(solution)/shard_map/ppermute | solution.py:349
  149.3 13.0 %collective-permute-start.25 = (f32[2,128]{1,0:T(2,128)S(1)}, f32[2,128]{1,0:T(2,128)S(1)}, u32[]{:S(2)}, u32[]{:S(2)}) collective-permute-start(f32[2,128]{1,0:T(2,128)S(1)} %bitcast.127), channel_id=1, source_target_pairs={{0,128},{64,192},{128,0},{192,64},{1,129},{65,193},{129,1},{193,65... | collective-permute-start | bytes 3080 | tf_op jit(solution)/shard_map/ppermute | solution.py:349
  (9 other events, 80.9 us)
where the time goes:
time: 167 us; the launch traced here: 164 us
  starting transfers between devices  63 us (38%)
  Pallas kernels  48.3 us (29%)
  waiting for transfers between devices  28.3 us (17%)
  local copies, waits for them, and re-layouts  12.3 us (7%)
  between operations  7.7 us (5%)
  other arithmetic  4.59 us (3%)
    ppermute x24, starting transfers between devices, send(): return lax.ppermute(x, 'tile', pairs)  49.3 us
    pallas_call x2, Pallas kernels, attend(): pl.pallas_call(functools.partial(attend_kernel, steps, last), grid_spec=p...  39 us
    ppermute x24, waiting for transfers between devices, send(): return lax.ppermute(x, 'tile', pairs)  26.9 us
    ppermute x3, starting transfers between devices, per_device(): lax.ppermute(gains, 'dp', [(i, (i + by) % 4) for i in range(4)])  13.8 us
    pallas_call x2, Pallas kernels, finish(): pl.pallas_call(finish_kernel, grid=(heads // 2,), in_specs=in_specs, out_...  9.3 us
    slice x6, local copies, waits for them, and re-layouts, after(): zero = jnp.minimum(jnp.abs(other[(-1,) * other.ndim]), 0).astype(x.dtype)  3.67 us
  transfers between devices with their start and end apart: 27, of which 7 were waited for; matrix products, arithmetic and copies ran while one was open for 9% of the time, Pallas kernels for 29%

commit v1 on v0

--- a/solution.py
+++ b/solution.py
@@ -302,15 +302,16 @@
 
 
 def reduce_text(mine, other, first, second):
-    total = mine + send(other, steps_along(3, -1))
+    total = mine + send(other.astype(BF16), steps_along(3, -1)).astype(F32)
     for dim in (1, 2, 0):
         if dim == 1:
             parts = [total[i] for i in range(4)]
         else:
-            total = after(total, *(first if dim == 2 else second))
+            total = after(total, *(list(first) + list(second[:1]) if dim == 2 else second[1:]))
             n = total.shape[1] // SIZES[dim]
             parts = [total[:, i * n : (i + 1) * n] for i in range(SIZES[dim])]
-        got = [send(parts[by], steps_along(dim, -by)) for by in range(1, SIZES[dim])]
+        kind = BF16 if dim == 1 else F32
+        got = [send(parts[by].astype(kind), steps_along(dim, -by)).astype(F32) for by in range(1, SIZES[dim])]
         total = functools.reduce(jnp.add, got, parts[0])
     return total[:, 0]
 

time: 167 us -> 167 us (level)
  the two profiles are of different devices: /device:TPU:31 before, /device:TPU:0 now
where the time goes in v1:
time: 167 us
  starting transfers between devices  69.8 us (42%)
  Pallas kernels  48.3 us (29%)
  waiting for transfers between devices  24.3 us (15%)
  local copies, waits for them, and re-layouts  12.2 us (7%)
  between operations  7.58 us (5%)
  other arithmetic  4.47 us (3%)
    ppermute x24, starting transfers between devices, send(): return lax.ppermute(x, 'tile', pairs)  52.5 us
    pallas_call x2, Pallas kernels, attend(): pl.pallas_call(functools.partial(attend_kernel, steps, last), grid_spec=p...  39 us
    ppermute x24, waiting for transfers between devices, send(): return lax.ppermute(x, 'tile', pairs)  21.5 us
    ppermute x3, starting transfers between devices, per_device(): lax.ppermute(gains, 'dp', [(i, (i + by) % 4) for i in range(4)])  17.3 us
    pallas_call x2, Pallas kernels, finish(): pl.pallas_call(finish_kernel, grid=(heads // 2,), in_specs=in_specs, out_...  9.29 us
    slice x6, local copies, waits for them, and re-layouts, after(): zero = jnp.minimum(jnp.abs(other[(-1,) * other.ndim]), 0).astype(x.dtype)  3.67 us
  transfers between devices with their start and end apart: 27, of which 8 were waited for; matrix products, arithmetic and copies ran while one was open for 8% of the time, Pallas kernels for 29%

profile of v1, /device:TPU:0, one launch (start us, length us, event | category | flops | bytes accessed | tf_op | source)
XLA Modules:
  0.0 166.6 jit_solution(16232259963877645798)
XLA Ops:
  1.4 5.5 %collective-permute-start = (bf16[1,48,128]{2,1,0:T(8,128)(2,1)S(1)}, bf16[1,48,128]{2,1,0:T(8,128)(2,1)S(1)}, u32[]{:S(2)}, u32[]{:S(2)}) collective-permute-start(bf16[1,48,128]{2,1,0:T(8,128)(2,1)S(1)} %bitcast.119), channel_id=1, source_target_pairs={{0,32},{1,33},{2,34},{3,35},{4,36},{5,37},{6,38},{7,39},{8,40},{9,... | collective-permute-start | bytes 36872 | tf_op jit(solution)/shard_map/ppermute | solution.py:273
  7.0 1.8 %slice_bitcast_fusion = (bf16[1,384,768]{2,1,0:T(8,128)(2,1)S(1)}, bf16[1,384,768]{2,1,0:T(8,128)(2,1)S(1)}, bf16[1,384,768]{2,1,0:T(8,128)(2,1)S(1)}, bf16[1,384,768]{2,1,0:T(8,128)(2,1)S(1)}) fusion(bf16[384,1536]{1,0:T(8,128)(2,1)} %bitcast.108, bf16[384,1536]{1,0:T(8,128)(2,1)} %bitcast.102), kind=kLoop, calls=%fused_computation.5 | loop fusion | bytes 4718592 | tf_op jit(solution)/shard_map/stack | solution.py:329
  10.5 1.7 %collective-permute-start.11 = (bf16[2,384,768]{2,1,0:T(8,128)(2,1)S(1)}, bf16[2,384,768]{2,1,0:T(8,128)(2,1)}, u32[]{:S(2)}, u32[]{:S(2)}) collective-permute-start(bf16[2,384,768]{2,1,0:T(8,128)(2,1)S(1)} %maximum_add_fusion.1), channel_id=1, source_target_pairs={{1,2},{2,1},{3,4},{4,3},{5,6},{6,5},{7,8},{8,7},{9,10},{10,9},{11,... | collective-permute-start | bytes 3538952 | tf_op jit(solution)/shard_map/ppermute | solution.py:273
  13.9 3.5 %collective-permute-start.2 = (bf16[2,48,128]{2,1,0:T(8,128)(2,1)S(1)}, bf16[2,48,128]{2,1,0:T(8,128)(2,1)S(1)}, u32[]{:S(2)}, u32[]{:S(2)}) collective-permute-start(bf16[2,48,128]{2,1,0:T(8,128)(2,1)S(1)} %get-tuple-element.65), channel_id=1, source_target_pairs={{0,16},{1,17},{2,18},{3,19},{4,20},{5,21},{6,22},{7,23},{8,24},{9,... | collective-permute-start | bytes 73736 | tf_op jit(solution)/shard_map/ppermute | solution.py:273
  18.3 2.4 %collective-permute-start.3 = (bf16[2,48,128]{2,1,0:T(8,128)(2,1)S(1)}, bf16[2,48,128]{2,1,0:T(8,128)(2,1)S(1)}, u32[]{:S(2)}, u32[]{:S(2)}) collective-permute-start(bf16[2,48,128]{2,1,0:T(8,128)(2,1)S(1)} %get-tuple-element.65), channel_id=1, source_target_pairs={{0,24},{1,25},{2,26},{3,27},{4,28},{5,29},{6,30},{7,31},{8,0},{9,1... | collective-permute-start | bytes 73736 | tf_op jit(solution)/shard_map/ppermute | solution.py:273
  23.2 7.7 %collective-permute-done.3 = bf16[2,48,128]{2,1,0:T(8,128)(2,1)S(1)} collective-permute-done((bf16[2,48,128]{2,1,0:T(8,128)(2,1)S(1)}, bf16[2,48,128]{2,1,0:T(8,128)(2,1)S(1)}, u32[]{:S(2)}, u32[]{:S(2)}) %collective-permute-start.3) | collective-permute-done | bytes 24608 | tf_op jit(solution)/shard_map/ppermute | solution.py:273
  31.1 1.9 %collective-permute-start.4 = (bf16[4,2,48,128]{3,2,1,0:T(8,128)(2,1)S(1)}, bf16[4,2,48,128]{3,2,1,0:T(8,128)(2,1)S(1)}, u32[]{:S(2)}, u32[]{:S(2)}) collective-permute-start(bf16[4,2,48,128]{3,2,1,0:T(8,128)(2,1)S(1)} %get-tuple-element.61), channel_id=1, source_target_pairs={{0,2},{1,3},{2,4},{3,5},{4,6},{5,7},{6,0},{7,1},{8,10},{9,11},{10,... | collective-permute-start | bytes 294920 | tf_op jit(solution)/shard_map/ppermute | solution.py:273
  33.0 3.4 %collective-permute-done.6 = bf16[4,2,48,128]{3,2,1,0:T(8,128)(2,1)S(1)} collective-permute-done((bf16[4,2,48,128]{3,2,1,0:T(8,128)(2,1)S(1)}, bf16[4,2,48,128]{3,2,1,0:T(8,128)(2,1)S(1)}, u32[]{:S(2)}, u32[]{:S(2)}) %collective-permute-start.6) | collective-permute-done | bytes 98336 | tf_op jit(solution)/shard_map/ppermute | solution.py:273
  42.8 1.7 %collective-permute-start.8 = (bf16[2,384,768]{2,1,0:T(8,128)(2,1)S(1)}, bf16[2,384,768]{2,1,0:T(8,128)(2,1)}, u32[]{:S(2)}, u32[]{:S(2)}) collective-permute-start(bf16[2,384,768]{2,1,0:T(8,128)(2,1)S(1)} %fusion.1), channel_id=1, source_target_pairs={{1,2},{2,1},{3,4},{4,3},{5,6},{6,5},{7,8},{8,7},{9,10},{10,9},{11,... | collective-permute-start | bytes 3538952 | tf_op jit(solution)/shard_map/ppermute | solution.py:273
  46.9 19.4 %shard_map.161 = (bf16[384,1536]{1,0:T(8,128)(2,1)}, bf16[384,1536]{1,0:T(8,128)(2,1)}, f32[2,384,768]{2,1,0:T(8,128)}, bf16[2,384,768]{2,1,0:T(8,128)(2,1)}, bf...) custom-call(s32[2]{0:T(128)} %add_convert_fusion.flags, ...), custom_call_target="tpu_custom_call" | custom-call | flops 9059696640 | bytes 5308416 | tf_op jit(solution)/shard_map/pallas_call | solution.py:209
  66.4 1.8 %collective-permute-start.15 = (bf16[2,384,768]{2,1,0:T(8,128)(2,1)}, bf16[2,384,768]{2,1,0:T(8,128)(2,1)}, u32[]{:S(2)}, u32[]{:S(2)}) collective-permute-start(bf16[2,384,768]{2,1,0:T(8,128)(2,1)} %get-tuple-element.39), channel_id=1, source_target_pairs={{1,2},{2,1},{3,4},{4,3},{5,6},{6,5},{7,8},{8,7},{9,10},{10,9},{11,... | collective-permute-start | bytes 3538952 | tf_op jit(solution)/shard_map/ppermute | solution.py:273
  68.2 19.6 %shard_map.162 = (bf16[384,1536]{1,0:T(8,128)(2,1)}, bf16[384,1536]{1,0:T(8,128)(2,1)}, f32[2,384,768]{2,1,0:T(8,128)}, bf16[2,384,768]{2,1,0:T(8,128)(2,1)}, bf...) custom-call(s32[2]{0:T(128)} %add_convert_fusion.flags, ...), custom_call_target="tpu_custom_call", output_to_operand_aliasing={{0}: (13, {}), {1}: (14, {}), {5}: (15, {}), {6}: (16, {})} | custom-call | flops 9059696640 | bytes 5308416 | tf_op jit(solution)/shard_map/pallas_call | solution.py:209
  87.8 2.5 %collective-permute-start.12 = (bf16[2,384,768]{2,1,0:T(8,128)(2,1)}, bf16[2,384,768]{2,1,0:T(8,128)(2,1)S(1)}, u32[]{:S(2)}, u32[]{:S(2)}) collective-permute-start(bf16[2,384,768]{2,1,0:T(8,128)(2,1)} %get-tuple-element.35), channel_id=1, source_target_pairs={{0,1},{1,0},{2,3},{3,2},{4,5},{5,4},{6,7},{7,6},{8,9},{9,8},{10,11... | collective-permute-start | bytes 3538952 | tf_op jit(solution)/shard_map/ppermute | solution.py:273
  94.3 6.8 %collective-permute-start.17 = (bf16[56,8,128]{2,1,0:T(8,128)(2,1)}, bf16[56,8,128]{2,1,0:T(8,128)(2,1)S(1)}, u32[]{:S(2)}, u32[]{:S(2)}) collective-permute-start(bf16[56,8,128]{2,1,0:T(8,128)(2,1)} %get-tuple-element.54), channel_id=1, source_target_pairs={{0,24},{1,25},{2,26},{3,27},{4,28},{5,29},{6,30},{7,31},{8,0},{9,1... | collective-permute-start | bytes 344072 | tf_op jit(solution)/shard_map/ppermute | solution.py:273
  101.1 1.6 collective-permute-start.18
  102.8 4.6 %shard_map.163 = (bf16[384,1536]{1,0:T(8,128)(2,1)}, bf16[384,1536]{1,0:T(8,128)(2,1)}) custom-call(bf16[384,1536]{1,0:T(8,128)(2,1)} %bitcast.105, f32[2,384,768]{2,1,0:T(8,128)} %get-tuple-element.37.own_ref, bf16[2,384,768]{2,1,0:T(8,128)(2,1)} %collective-permute-done.14.a_ref, bf16[2,384,768]{2,1,0:T(8,128)(2,1)} %collective-permute-done.15.b_ref, ...), custom_call_target="tpu_custom_call" | custom-call | flops 5898240 | bytes 7667712 | tf_op jit(solution)/shard_map/pallas_call | solution.py:260
  110.6 4.7 %collective-permute-done.17 = bf16[56,8,128]{2,1,0:T(8,128)(2,1)S(1)} collective-permute-done((bf16[56,8,128]{2,1,0:T(8,128)(2,1)}, bf16[56,8,128]{2,1,0:T(8,128)(2,1)S(1)}, u32[]{:S(2)}, u32[]{:S(2)}) %collective-permute-start.17) | collective-permute-done | bytes 114720 | tf_op jit(solution)/shard_map/ppermute | solution.py:273
  117.1 5.0 %collective-permute-start.20 = (f32[56,2,128]{2,1,0:T(2,128)S(1)}, f32[56,2,128]{2,1,0:T(2,128)S(1)}, u32[]{:S(2)}, u32[]{:S(2)}) collective-permute-start(f32[56,2,128]{2,1,0:T(2,128)S(1)} %get-tuple-element.57), channel_id=1, source_target_pairs={{0,6},{1,7},{2,0},{3,1},{4,2},{5,3},{6,4},{7,5},{8,14},{9,15},{10,... | collective-permute-start | bytes 172040 | tf_op jit(solution)/shard_map/ppermute | solution.py:273
  125.1 3.1 %collective-permute-done.22 = f32[56,2,128]{2,1,0:T(2,128)S(1)} collective-permute-done((f32[56,2,128]{2,1,0:T(2,128)S(1)}, f32[56,2,128]{2,1,0:T(2,128)S(1)}, u32[]{:S(2)}, u32[]{:S(2)}) %collective-permute-start.22) | collective-permute-done | bytes 57376 | tf_op jit(solution)/shard_map/ppermute | solution.py:273
  128.2 11.5 %collective-permute-start.23 = (f32[56,1,128]{2,1,0:T(1,128)S(1)}, f32[56,1,128]{2,1,0:T(1,128)S(1)}, u32[]{:S(2)}, u32[]{:S(2)}) collective-permute-start(f32[56,1,128]{2,1,0:T(1,128)S(1)} %slice.146), channel_id=1, source_target_pairs={{0,32},{1,33},{2,34},{3,35},{4,36},{5,37},{6,38},{7,39},{8,40},{9,... | collective-permute-start | bytes 86024 | tf_op jit(solution)/shard_map/ppermute | solution.py:273
  139.8 4.7 %shard_map.164 = (bf16[384,1536]{1,0:T(8,128)(2,1)}, bf16[384,1536]{1,0:T(8,128)(2,1)}) custom-call(bf16[384,1536]{1,0:T(8,128)(2,1)} %bitcast.106, f32[2,384,768]{2,1,0:T(8,128)} %get-tuple-element.34.own_ref, bf16[2,384,768]{2,1,0:T(8,128)(2,1)} %copy-done.1, bf16[2,384,768]{2,1,0:T(8,128)(2,1)} %copy-done.2, ...), custom_call_target="tpu_custom_call", output_to_operand_aliasing={{0}: (5, {}), {1}: (6, {})} | custom-call | flops 5898240 | bytes 7667712 | tf_op jit(solution)/shard_map/pallas_call | solution.py:260
  144.6 2.0 %collective-permute-start.26 = (f32[2,128]{1,0:T(2,128)S(1)}, f32[2,128]{1,0:T(2,128)S(1)}, u32[]{:S(2)}, u32[]{:S(2)}) collective-permute-start(f32[2,128]{1,0:T(2,128)S(1)} %bitcast.128), channel_id=1, source_target_pairs={{0,192},{64,0},{128,64},{192,128},{1,193},{65,1},{129,65},{193,129... | collective-permute-start | bytes 3080 | tf_op jit(solution)/shard_map/ppermute | solution.py:350
  146.6 14.2 %collective-permute-start.25 = (f32[2,128]{1,0:T(2,128)S(1)}, f32[2,128]{1,0:T(2,128)S(1)}, u32[]{:S(2)}, u32[]{:S(2)}) collective-permute-start(f32[2,128]{1,0:T(2,128)S(1)} %bitcast.129), channel_id=1, source_target_pairs={{0,128},{64,192},{128,0},{192,64},{1,129},{65,193},{129,1},{193,65... | collective-permute-start | bytes 3080 | tf_op jit(solution)/shard_map/ppermute | solution.py:350
  163.3 2.8 %collective-permute-done.24 = f32[2,128]{1,0:T(2,128)S(1)} collective-permute-done((f32[2,128]{1,0:T(2,128)S(1)}, f32[2,128]{1,0:T(2,128)S(1)}, u32[]{:S(2)}, u32[]{:S(2)}) %collective-permute-start.24) | collective-permute-done | bytes 1056 | tf_op jit(solution)/shard_map/ppermute | solution.py:350
  (95 shorter events, 25.2 us)
Async XLA Ops:
  1.4 7.7 %collective-permute-start = (bf16[1,48,128]{2,1,0:T(8,128)(2,1)S(1)}, bf16[1,48,128]{2,1,0:T(8,128)(2,1)S(1)}, u32[]{:S(2)}, u32[]{:S(2)}) collective-permute-start(bf16[1,48,128]{2,1,0:T(8,128)(2,1)S(1)} %bitcast.119), channel_id=1, source_target_pairs={{0,32},{1,33},{2,34},{3,35},{4,36},{5,37},{6,38},{7,39},{8,40},{9,... | collective-permute-start | bytes 36872 | tf_op jit(solution)/shard_map/ppermute | solution.py:273
  10.5 36.4 %collective-permute-start.11 = (bf16[2,384,768]{2,1,0:T(8,128)(2,1)S(1)}, bf16[2,384,768]{2,1,0:T(8,128)(2,1)}, u32[]{:S(2)}, u32[]{:S(2)}) collective-permute-start(bf16[2,384,768]{2,1,0:T(8,128)(2,1)S(1)} %maximum_add_fusion.1), channel_id=1, source_target_pairs={{1,2},{2,1},{3,4},{4,3},{5,6},{6,5},{7,8},{8,7},{9,10},{10,9},{11,... | collective-permute-start | bytes 3538952 | tf_op jit(solution)/shard_map/ppermute | solution.py:273
  12.2 34.7 %collective-permute-start.10 = (bf16[2,384,768]{2,1,0:T(8,128)(2,1)S(1)}, bf16[2,384,768]{2,1,0:T(8,128)(2,1)}, u32[]{:S(2)}, u32[]{:S(2)}) collective-permute-start(bf16[2,384,768]{2,1,0:T(8,128)(2,1)S(1)} %maximum_add_fusion.1), channel_id=1, source_target_pairs={{0,1},{1,0},{2,3},{3,2},{4,5},{5,4},{6,7},{7,6},{8,9},{9,8},{10,11... | collective-permute-start | bytes 3538952 | tf_op jit(solution)/shard_map/ppermute | solution.py:273
  13.9 9.3 %collective-permute-start.2 = (bf16[2,48,128]{2,1,0:T(8,128)(2,1)S(1)}, bf16[2,48,128]{2,1,0:T(8,128)(2,1)S(1)}, u32[]{:S(2)}, u32[]{:S(2)}) collective-permute-start(bf16[2,48,128]{2,1,0:T(8,128)(2,1)S(1)} %get-tuple-element.65), channel_id=1, source_target_pairs={{0,16},{1,17},{2,18},{3,19},{4,20},{5,21},{6,22},{7,23},{8,24},{9,... | collective-permute-start | bytes 73736 | tf_op jit(solution)/shard_map/ppermute | solution.py:273
  17.4 5.7 %collective-permute-start.1 = (bf16[2,48,128]{2,1,0:T(8,128)(2,1)S(1)}, bf16[2,48,128]{2,1,0:T(8,128)(2,1)S(1)}, u32[]{:S(2)}, u32[]{:S(2)}) collective-permute-start(bf16[2,48,128]{2,1,0:T(8,128)(2,1)S(1)} %get-tuple-element.65), channel_id=1, source_target_pairs={{0,8},{1,9},{2,10},{3,11},{4,12},{5,13},{6,14},{7,15},{8,16},{9,17... | collective-permute-start | bytes 73736 | tf_op jit(solution)/shard_map/ppermute | solution.py:273
  18.3 12.6 %collective-permute-start.3 = (bf16[2,48,128]{2,1,0:T(8,128)(2,1)S(1)}, bf16[2,48,128]{2,1,0:T(8,128)(2,1)S(1)}, u32[]{:S(2)}, u32[]{:S(2)}) collective-permute-start(bf16[2,48,128]{2,1,0:T(8,128)(2,1)S(1)} %get-tuple-element.65), channel_id=1, source_target_pairs={{0,24},{1,25},{2,26},{3,27},{4,28},{5,29},{6,30},{7,31},{8,0},{9,1... | collective-permute-start | bytes 73736 | tf_op jit(solution)/shard_map/ppermute | solution.py:273
  30.9 5.5 %collective-permute-start.6 = (bf16[4,2,48,128]{3,2,1,0:T(8,128)(2,1)S(1)}, bf16[4,2,48,128]{3,2,1,0:T(8,128)(2,1)S(1)}, u32[]{:S(2)}, u32[]{:S(2)}) collective-permute-start(bf16[4,2,48,128]{3,2,1,0:T(8,128)(2,1)S(1)} %get-tuple-element.61), channel_id=1, source_target_pairs={{0,6},{1,7},{2,0},{3,1},{4,2},{5,3},{6,4},{7,5},{8,14},{9,15},{10,... | collective-permute-start | bytes 294920 | tf_op jit(solution)/shard_map/ppermute | solution.py:273
  31.0 6.7 %collective-permute-start.5 = (bf16[4,2,48,128]{3,2,1,0:T(8,128)(2,1)S(1)}, bf16[4,2,48,128]{3,2,1,0:T(8,128)(2,1)S(1)}, u32[]{:S(2)}, u32[]{:S(2)}) collective-permute-start(bf16[4,2,48,128]{3,2,1,0:T(8,128)(2,1)S(1)} %get-tuple-element.61), channel_id=1, source_target_pairs={{0,4},{1,5},{2,6},{3,7},{4,0},{5,1},{6,2},{7,3},{8,12},{9,13},{10,... | collective-permute-start | bytes 294920 | tf_op jit(solution)/shard_map/ppermute | solution.py:273
  31.1 9.3 %collective-permute-start.4 = (bf16[4,2,48,128]{3,2,1,0:T(8,128)(2,1)S(1)}, bf16[4,2,48,128]{3,2,1,0:T(8,128)(2,1)S(1)}, u32[]{:S(2)}, u32[]{:S(2)}) collective-permute-start(bf16[4,2,48,128]{3,2,1,0:T(8,128)(2,1)S(1)} %get-tuple-element.61), channel_id=1, source_target_pairs={{0,2},{1,3},{2,4},{3,5},{4,6},{5,7},{6,0},{7,1},{8,10},{9,11},{10,... | collective-permute-start | bytes 294920 | tf_op jit(solution)/shard_map/ppermute | solution.py:273
  42.8 25.4 %collective-permute-start.8 = (bf16[2,384,768]{2,1,0:T(8,128)(2,1)S(1)}, bf16[2,384,768]{2,1,0:T(8,128)(2,1)}, u32[]{:S(2)}, u32[]{:S(2)}) collective-permute-start(bf16[2,384,768]{2,1,0:T(8,128)(2,1)S(1)} %fusion.1), channel_id=1, source_target_pairs={{1,2},{2,1},{3,4},{4,3},{5,6},{6,5},{7,8},{8,7},{9,10},{10,9},{11,... | collective-permute-start | bytes 3538952 | tf_op jit(solution)/shard_map/ppermute | solution.py:273
  44.5 23.7 %collective-permute-start.7 = (bf16[2,384,768]{2,1,0:T(8,128)(2,1)S(1)}, bf16[2,384,768]{2,1,0:T(8,128)(2,1)}, u32[]{:S(2)}, u32[]{:S(2)}) collective-permute-start(bf16[2,384,768]{2,1,0:T(8,128)(2,1)S(1)} %fusion.1), channel_id=1, source_target_pairs={{0,1},{1,0},{2,3},{3,2},{4,5},{5,4},{6,7},{7,6},{8,9},{9,8},{10,11... | collective-permute-start | bytes 3538952 | tf_op jit(solution)/shard_map/ppermute | solution.py:273
  66.3 34.9 %collective-permute-start.14 = (bf16[2,384,768]{2,1,0:T(8,128)(2,1)}, bf16[2,384,768]{2,1,0:T(8,128)(2,1)}, u32[]{:S(2)}, u32[]{:S(2)}) collective-permute-start(bf16[2,384,768]{2,1,0:T(8,128)(2,1)} %get-tuple-element.38), channel_id=1, source_target_pairs={{0,1},{1,0},{2,3},{3,2},{4,5},{5,4},{6,7},{7,6},{8,9},{9,8},{10,11... | collective-permute-start | bytes 3538952 | tf_op jit(solution)/shard_map/ppermute | solution.py:273
  66.4 34.7 %collective-permute-start.15 = (bf16[2,384,768]{2,1,0:T(8,128)(2,1)}, bf16[2,384,768]{2,1,0:T(8,128)(2,1)}, u32[]{:S(2)}, u32[]{:S(2)}) collective-permute-start(bf16[2,384,768]{2,1,0:T(8,128)(2,1)} %get-tuple-element.39), channel_id=1, source_target_pairs={{1,2},{2,1},{3,4},{4,3},{5,6},{6,5},{7,8},{8,7},{9,10},{10,9},{11,... | collective-permute-start | bytes 3538952 | tf_op jit(solution)/shard_map/ppermute | solution.py:273
  87.8 21.5 %collective-permute-start.12 = (bf16[2,384,768]{2,1,0:T(8,128)(2,1)}, bf16[2,384,768]{2,1,0:T(8,128)(2,1)S(1)}, u32[]{:S(2)}, u32[]{:S(2)}) collective-permute-start(bf16[2,384,768]{2,1,0:T(8,128)(2,1)} %get-tuple-element.35), channel_id=1, source_target_pairs={{0,1},{1,0},{2,3},{3,2},{4,5},{5,4},{6,7},{7,6},{8,9},{9,8},{10,11... | collective-permute-start | bytes 3538952 | tf_op jit(solution)/shard_map/ppermute | solution.py:273
  91.7 32.0 %collective-permute-start.13 = (bf16[2,384,768]{2,1,0:T(8,128)(2,1)}, bf16[2,384,768]{2,1,0:T(8,128)(2,1)S(1)}, u32[]{:S(2)}, u32[]{:S(2)}) collective-permute-start(bf16[2,384,768]{2,1,0:T(8,128)(2,1)} %get-tuple-element.36), channel_id=1, source_target_pairs={{1,2},{2,1},{3,4},{4,3},{5,6},{6,5},{7,8},{8,7},{9,10},{10,9},{11,... | collective-permute-start | bytes 3538952 | tf_op jit(solution)/shard_map/ppermute | solution.py:273
  94.3 21.0 %collective-permute-start.17 = (bf16[56,8,128]{2,1,0:T(8,128)(2,1)}, bf16[56,8,128]{2,1,0:T(8,128)(2,1)S(1)}, u32[]{:S(2)}, u32[]{:S(2)}) collective-permute-start(bf16[56,8,128]{2,1,0:T(8,128)(2,1)} %get-tuple-element.54), channel_id=1, source_target_pairs={{0,24},{1,25},{2,26},{3,27},{4,28},{5,29},{6,30},{7,31},{8,0},{9,1... | collective-permute-start | bytes 344072 | tf_op jit(solution)/shard_map/ppermute | solution.py:273
  101.1 14.2 %collective-permute-start.19 = (bf16[56,8,128]{2,1,0:T(8,128)(2,1)}, bf16[56,8,128]{2,1,0:T(8,128)(2,1)S(1)}, u32[]{:S(2)}, u32[]{:S(2)}) collective-permute-start(bf16[56,8,128]{2,1,0:T(8,128)(2,1)} %get-tuple-element.55), channel_id=1, source_target_pairs={{0,8},{1,9},{2,10},{3,11},{4,12},{5,13},{6,14},{7,15},{8,16},{9,17... | collective-permute-start | bytes 344072 | tf_op jit(solution)/shard_map/ppermute | solution.py:273
  101.1 14.2 %collective-permute-start.18 = (bf16[56,8,128]{2,1,0:T(8,128)(2,1)}, bf16[56,8,128]{2,1,0:T(8,128)(2,1)}, u32[]{:S(2)}, u32[]{:S(2)}) collective-permute-start(bf16[56,8,128]{2,1,0:T(8,128)(2,1)} %get-tuple-element.56), channel_id=1, source_target_pairs={{0,16},{1,17},{2,18},{3,19},{4,20},{5,21},{6,22},{7,23},{8,24},{9,... | collective-permute-start | bytes 344072 | tf_op jit(solution)/shard_map/ppermute | solution.py:273
  117.1 7.9 %collective-permute-start.20 = (f32[56,2,128]{2,1,0:T(2,128)S(1)}, f32[56,2,128]{2,1,0:T(2,128)S(1)}, u32[]{:S(2)}, u32[]{:S(2)}) collective-permute-start(f32[56,2,128]{2,1,0:T(2,128)S(1)} %get-tuple-element.57), channel_id=1, source_target_pairs={{0,6},{1,7},{2,0},{3,1},{4,2},{5,3},{6,4},{7,5},{8,14},{9,15},{10,... | collective-permute-start | bytes 172040 | tf_op jit(solution)/shard_map/ppermute | solution.py:273
  122.1 6.0 %collective-permute-start.22 = (f32[56,2,128]{2,1,0:T(2,128)S(1)}, f32[56,2,128]{2,1,0:T(2,128)S(1)}, u32[]{:S(2)}, u32[]{:S(2)}) collective-permute-start(f32[56,2,128]{2,1,0:T(2,128)S(1)} %get-tuple-element.58), channel_id=1, source_target_pairs={{0,2},{1,3},{2,4},{3,5},{4,6},{5,7},{6,0},{7,1},{8,10},{9,11},{10,... | collective-permute-start | bytes 172040 | tf_op jit(solution)/shard_map/ppermute | solution.py:273
  122.1 6.0 %collective-permute-start.21 = (f32[56,2,128]{2,1,0:T(2,128)S(1)}, f32[56,2,128]{2,1,0:T(2,128)S(1)}, u32[]{:S(2)}, u32[]{:S(2)}) collective-permute-start(f32[56,2,128]{2,1,0:T(2,128)S(1)} %get-tuple-element.59), channel_id=1, source_target_pairs={{0,4},{1,5},{2,6},{3,7},{4,0},{5,1},{6,2},{7,3},{8,12},{9,13},{10,... | collective-permute-start | bytes 172040 | tf_op jit(solution)/shard_map/ppermute | solution.py:273
  128.2 16.3 %collective-permute-start.23 = (f32[56,1,128]{2,1,0:T(1,128)S(1)}, f32[56,1,128]{2,1,0:T(1,128)S(1)}, u32[]{:S(2)}, u32[]{:S(2)}) collective-permute-start(f32[56,1,128]{2,1,0:T(1,128)S(1)} %slice.146), channel_id=1, source_target_pairs={{0,32},{1,33},{2,34},{3,35},{4,36},{5,37},{6,38},{7,39},{8,40},{9,... | collective-permute-start | bytes 86024 | tf_op jit(solution)/shard_map/ppermute | solution.py:273
  144.6 18.8 %collective-permute-start.26 = (f32[2,128]{1,0:T(2,128)S(1)}, f32[2,128]{1,0:T(2,128)S(1)}, u32[]{:S(2)}, u32[]{:S(2)}) collective-permute-start(f32[2,128]{1,0:T(2,128)S(1)} %bitcast.128), channel_id=1, source_target_pairs={{0,192},{64,0},{128,64},{192,128},{1,193},{65,1},{129,65},{193,129... | collective-permute-start | bytes 3080 | tf_op jit(solution)/shard_map/ppermute | solution.py:350
  146.6 16.8 %collective-permute-start.25 = (f32[2,128]{1,0:T(2,128)S(1)}, f32[2,128]{1,0:T(2,128)S(1)}, u32[]{:S(2)}, u32[]{:S(2)}) collective-permute-start(f32[2,128]{1,0:T(2,128)S(1)} %bitcast.129), channel_id=1, source_target_pairs={{0,128},{64,192},{128,0},{192,64},{1,129},{65,193},{129,1},{193,65... | collective-permute-start | bytes 3080 | tf_op jit(solution)/shard_map/ppermute | solution.py:350
  (11 other events, 132.8 us)
